TPU v7x, 128 devices: a whole 4x4x4 slice. The times are simulated.
128 devices in a mesh: row: 8 (over y, core), col: 16 (over z, x).
Axes of the slice: x: 4, y: 4, z: 4, core: 2. Of those that a mesh axis runs over, the one named last changes fastest.
Arguments:
- block_x: float32 [64, 98304], P(None, ('row', 'col')), may hold values from -6 to 6
- block_p: float32 [64, 98304], P(None, ('row', 'col')), may hold values from -6 to 6
- tile_rows: int32 [8, 16, 576], P('row', 'col'), may hold values from 0 to 95, as said below
- tile_cols: int32 [8, 16, 576], P('row', 'col'), may hold values from 0 to 47, as said below
- tile_count: int32 [8, 16], P('row', 'col'), may hold values from 1 to 576, as said below
- tile_vals: bfloat16 [8, 16, 576, 128, 128], P('row', 'col'), may hold values from -0.125 to 0.125
Outputs:
- residual: float32 [64, 98304], P(None, ('row', 'col'))
- image_r: float32 [64, 98304], P(None, ('row', 'col'))
- gram_a: float32 [192, 192], replicated
- gram_b: float32 [192, 192], replicated
Inputs may be any that keep to these rules, and one draw needn't show every extreme that they name: `tile_rows`: within one grid cell the live slots name distinct tiles, all with i <= j; slots at and beyond the cell's count are ignored. `tile_cols`: paired with tile_rows slot by slot. `tile_count`: some grid cell is full in every draw.
All inputs are finite; a program needn't handle non-finite values.
Results may differ from a plain program's by a relative error of at most 0.0035.
Values may be sent and summed in bfloat16 or wider, within the bound.
A program may use at most 128 MiB of HBM per device.

v0:
```python
import math
import jax
import jax.numpy as jnp
from jax import lax
from jax.sharding import PartitionSpec as P


def apply_graph(vectors, tile_rows, tile_cols, live_count, tile_vals):
    vec_width = vectors.shape[0]
    tile_size = tile_vals.shape[-1]
    row_range = lax.all_gather(vectors, "col", axis=1, tiled=True)
    col_group = lax.all_gather(vectors, "row", axis=1, tiled=True)
    row_blocks = row_range.reshape(vec_width, -1, tile_size)
    col_blocks = col_group.reshape(vec_width, -1, tile_size)
    group_size = math.gcd(tile_vals.shape[0], 64)
    offsets = jnp.arange(group_size, dtype=jnp.int32)
    turn_count = (live_count + group_size - 1) // group_size

    def slot_group(turn_index):
        first_slot = turn_index * group_size
        row_index = lax.dynamic_slice_in_dim(tile_rows, first_slot, group_size)
        col_index = lax.dynamic_slice_in_dim(tile_cols, first_slot, group_size)
        values = lax.dynamic_slice_in_dim(tile_vals, first_slot, group_size, 0)
        live_slots = first_slot + offsets < live_count
        return (row_index, col_index, values, live_slots)

    def turn(turn_index, totals):
        row_totals, col_totals = totals
        row_index, col_index, values, live_slots = slot_group(turn_index)
        values = jnp.where(live_slots[:, None, None], values, jnp.zeros_like(values))
        col_inputs = jnp.take(col_blocks, col_index, axis=1)
        row_inputs = jnp.take(row_blocks, row_index, axis=1)
        forward = jnp.einsum("wgb,gab->wga", col_inputs, values, preferred_element_type=jnp.float32)
        backward = jnp.einsum(
            "wga,gab->wgb", row_inputs, values, preferred_element_type=jnp.float32
        )
        return (row_totals.at[:, row_index].add(forward), col_totals.at[:, col_index].add(backward))

    start_rows = jnp.zeros(row_blocks.shape, jnp.float32)
    start_cols = jnp.zeros(col_blocks.shape, jnp.float32)
    row_totals, col_totals = lax.fori_loop(0, turn_count, turn, (start_rows, start_cols))
    own_rows = lax.psum_scatter(
        row_totals.reshape(vec_width, -1), "col", scatter_dimension=1, tiled=True
    )
    own_cols = lax.psum_scatter(
        col_totals.reshape(vec_width, -1), "row", scatter_dimension=1, tiled=True
    )
    return own_rows + own_cols


def per_device(block_x, block_p, tile_rows, tile_cols, tile_count, tile_vals):
    highest = lax.Precision.HIGHEST
    width_k = block_x.shape[0]
    node_count = block_x.shape[1] * lax.axis_size("row") * lax.axis_size("col")
    slot_rows = tile_rows[0, 0]
    slot_cols = tile_cols[0, 0]
    live_count = tile_count[0, 0]
    slot_vals = tile_vals[0, 0]

    def product(left, right):
        return (
            jnp.dot(left, right.T, precision=highest, preferred_element_type=jnp.float32)
            / node_count
        )

    gram_x = lax.psum(product(block_x, block_x), ("row", "col"))
    cholesky_factor = jnp.linalg.cholesky(gram_x)
    orthonormal = lax.linalg.triangular_solve(cholesky_factor, block_x, left_side=True, lower=True)
    ortho_low = orthonormal.astype(jnp.bfloat16)
    dir_low = block_p.astype(jnp.bfloat16)
    both_images = apply_graph(
        jnp.concatenate([ortho_low, dir_low], axis=0), slot_rows, slot_cols, live_count, slot_vals
    )
    image_x = both_images[:width_k]
    image_p = both_images[width_k:]
    rayleigh = lax.psum(product(orthonormal, image_x), ("row", "col"))
    residual = image_x - jnp.dot(
        rayleigh.T, orthonormal, precision=highest, preferred_element_type=jnp.float32
    )
    residual_low = residual.astype(jnp.bfloat16)
    image_r = apply_graph(residual_low, slot_rows, slot_cols, live_count, slot_vals)
    basis = jnp.concatenate([orthonormal, residual, block_p], axis=0)
    images = jnp.concatenate([image_x, image_r, image_p], axis=0)
    gram_a, gram_b = lax.psum((product(basis, images), product(basis, basis)), ("row", "col"))
    return (residual, image_r, gram_a, gram_b)


def solution(mesh):
    in_specs = (
        P(None, ("row", "col")),
        P(None, ("row", "col")),
        P("row", "col", None),
        P("row", "col", None),
        P("row", "col"),
        P("row", "col", None, None, None),
    )
    out_specs = (P(None, ("row", "col")), P(None, ("row", "col")), P(), P())
    return jax.shard_map(
        per_device, mesh=mesh, in_specs=in_specs, out_specs=out_specs, check_vma=False
    )
```

profile of v0, /device:TPU:1, one launch (start us, length us, event | category | flops | bytes accessed | tf_op | source)
XLA Modules:
  0.0 1301.9 jit_solution(9293041823528149920)
XLA Ops:
  8.4 68.9 %psum.28 = f32[64,64]{0,1:T(8,128)S(1)} all-reduce(f32[64,64]{0,1:T(8,128)S(1)} %convolution_multiply_fusion.3), channel_id=1, replica_groups=mesh['row'=8,'col'=16] {'row','col'}, use_global_device_ids=true, to_apply=%region_0.0 | all-reduce | flops 4096 | bytes 32768 | tf_op jit(solution)/shard_map/psum | solution.py:66
  77.4 5.8 cholesky.16
  84.6 4.9 custom-call.6
  93.1 19.8 %all-gather.4.cloned.1.call-done = bf16[128,6144]{1,0:T(8,128)(2,1)} async-done(((bf16[128,768]{1,0:T(8,128)(2,1)}), bf16[128,6144]{1,0:T(8,128)(2,1)}) %all-gather.4.cloned.1.call-update) | async-done | bytes 1572880 | tf_op jit(solution)/shard_map/all_gather | solution.py:12
  115.9 47.5 %all-gather.6.cloned.1.call-done = bf16[128,12288]{1,0:T(8,128)(2,1)} async-done(((bf16[128,768]{1,0:T(8,128)(2,1)}), bf16[128,12288]{1,0:T(8,128)(2,1)}) %all-gather.6.cloned.1.call-update) | async-done | bytes 3145744 | tf_op jit(solution)/shard_map/all_gather | solution.py:11
  163.3 4.5 copy_bitcast_fusion.3
  171.6 290.6 %while.26 = (s32[]{:T(128)}, f32[128,96,128]{2,0,1:T(8,128)}, f32[128,48,128]{2,0,1:T(8,128)S(1)}, s32[]{:T(128)}, s32[576]{0:T(1024)S(1)}, /*index=5*/s32[]{:T(...) while((s32[]{:T(128)}, f32[128,96,128]{2,0,1:T(8,128)}, ...), condition=%wide.region_6.7_spmd.clone, body=%wide.region_3.6_spmd.clone.sunk | while | flops 543165312 | bytes 50343056 | solution.py:41
  175.9 5.8 fusion.80
  181.7 13.6 %scatter_fusion = f32[128,96,128]{2,0,1:T(8,128)} fusion(f32[128,96,128]{2,0,1:T(8,128)} %get-tuple-element.407, s32[64]{0:T(128)S(1)} %get-tuple-element.374, f32[64,128,128]{2,1,0:T(8,128)} %fusion.80), kind=kCustom, calls=%fused_computation.4.clone.clone.1 | custom fusion | flops 1048576 | bytes 12583168 | tf_op jit(solution)/shard_map/while/body/scatter-add | solution.py:37
  195.4 4.0 gather_fusion.1
  199.4 4.9 fusion.81
  204.3 8.8 scatter_fusion.1
  217.4 5.8 fusion.80
  223.2 13.6 %scatter_fusion = f32[128,96,128]{2,0,1:T(8,128)} fusion(f32[128,96,128]{2,0,1:T(8,128)} %get-tuple-element.407, s32[64]{0:T(128)S(1)} %get-tuple-element.374, f32[64,128,128]{2,1,0:T(8,128)} %fusion.80), kind=kCustom, calls=%fused_computation.4.clone.clone.1 | custom fusion | flops 1048576 | bytes 12583168 | tf_op jit(solution)/shard_map/while/body/scatter-add | solution.py:37
  236.9 4.0 gather_fusion.1
  240.9 4.9 fusion.81
  245.8 8.8 scatter_fusion.1
  258.9 5.8 fusion.80
  264.8 13.6 %scatter_fusion = f32[128,96,128]{2,0,1:T(8,128)} fusion(f32[128,96,128]{2,0,1:T(8,128)} %get-tuple-element.407, s32[64]{0:T(128)S(1)} %get-tuple-element.374, f32[64,128,128]{2,1,0:T(8,128)} %fusion.80), kind=kCustom, calls=%fused_computation.4.clone.clone.1 | custom fusion | flops 1048576 | bytes 12583168 | tf_op jit(solution)/shard_map/while/body/scatter-add | solution.py:37
  278.4 4.0 gather_fusion.1
  282.4 4.9 fusion.81
  287.3 8.8 scatter_fusion.1
  300.5 5.8 fusion.80
  306.3 13.5 %scatter_fusion = f32[128,96,128]{2,0,1:T(8,128)} fusion(f32[128,96,128]{2,0,1:T(8,128)} %get-tuple-element.407, s32[64]{0:T(128)S(1)} %get-tuple-element.374, f32[64,128,128]{2,1,0:T(8,128)} %fusion.80), kind=kCustom, calls=%fused_computation.4.clone.clone.1 | custom fusion | flops 1048576 | bytes 12583168 | tf_op jit(solution)/shard_map/while/body/scatter-add | solution.py:37
  319.8 4.0 gather_fusion.1
  323.9 4.9 fusion.81
  328.8 8.8 scatter_fusion.1
  341.9 5.8 fusion.80
  347.7 13.6 %scatter_fusion = f32[128,96,128]{2,0,1:T(8,128)} fusion(f32[128,96,128]{2,0,1:T(8,128)} %get-tuple-element.407, s32[64]{0:T(128)S(1)} %get-tuple-element.374, f32[64,128,128]{2,1,0:T(8,128)} %fusion.80), kind=kCustom, calls=%fused_computation.4.clone.clone.1 | custom fusion | flops 1048576 | bytes 12583168 | tf_op jit(solution)/shard_map/while/body/scatter-add | solution.py:37
  361.3 4.0 gather_fusion.1
  365.4 4.9 fusion.81
  370.3 8.8 scatter_fusion.1
  383.4 5.8 fusion.80
  389.2 13.6 %scatter_fusion = f32[128,96,128]{2,0,1:T(8,128)} fusion(f32[128,96,128]{2,0,1:T(8,128)} %get-tuple-element.407, s32[64]{0:T(128)S(1)} %get-tuple-element.374, f32[64,128,128]{2,1,0:T(8,128)} %fusion.80), kind=kCustom, calls=%fused_computation.4.clone.clone.1 | custom fusion | flops 1048576 | bytes 12583168 | tf_op jit(solution)/shard_map/while/body/scatter-add | solution.py:37
  406.9 4.9 fusion.81
  411.8 8.8 scatter_fusion.1
  424.9 5.8 fusion.80
  430.7 13.6 %scatter_fusion = f32[128,96,128]{2,0,1:T(8,128)} fusion(f32[128,96,128]{2,0,1:T(8,128)} %get-tuple-element.407, s32[64]{0:T(128)S(1)} %get-tuple-element.374, f32[64,128,128]{2,1,0:T(8,128)} %fusion.80), kind=kCustom, calls=%fused_computation.4.clone.clone.1 | custom fusion | flops 1048576 | bytes 12583168 | tf_op jit(solution)/shard_map/while/body/scatter-add | solution.py:37
  448.4 4.9 fusion.81
  453.3 8.8 scatter_fusion.1
  464.2 6.1 copy_bitcast_fusion
  470.4 106.4 %reduce-scatter.7.cloned.1.call-done = f32[128,768]{1,0:T(8,128)} async-done(((f32[128,6144]{1,0:T(8,128)}), f32[128,768]{1,0:T(8,128)}) %reduce-scatter.7.cloned.1.call-update) | async-done | bytes 393232 | tf_op jit(solution)/shard_map/reduce_scatter | solution.py:45
  576.8 85.4 %reduce-scatter.5.cloned.1.call-done = f32[128,768]{1,0:T(8,128)} async-done(((f32[128,12288]{1,0:T(8,128)}), f32[128,768]{1,0:T(8,128)}) %reduce-scatter.5.cloned.1.call-update) | async-done | bytes 393232 | tf_op jit(solution)/shard_map/reduce_scatter | solution.py:42
  663.6 65.7 %psum.29 = f32[64,64]{0,1:T(8,128)S(1)} all-reduce(f32[64,64]{0,1:T(8,128)S(1)} %convolution_multiply_fusion.2), channel_id=1, replica_groups=mesh['row'=8,'col'=16] {'row','col'}, use_global_device_ids=true, to_apply=%region_9.10 | all-reduce | flops 4096 | bytes 32768 | tf_op jit(solution)/shard_map/psum | solution.py:76
  730.4 14.3 %all_gather.14 = bf16[64,6144]{1,0:T(8,128)(2,1)S(1)} all-gather(bf16[64,768]{1,0:T(8,128)(2,1)} %get-tuple-element.250), channel_id=1, replica_groups=mesh['row'=8,'col'=16] {'row'}, dimensions={1}, use_global_device_ids=true | all-gather | bytes 884736 | tf_op jit(solution)/shard_map/all_gather | solution.py:12
  745.8 24.0 %all-gather.8.cloned.1.call-done = bf16[64,12288]{1,0:T(8,128)(2,1)} async-done(((bf16[64,768]{1,0:T(8,128)(2,1)}), bf16[64,12288]{1,0:T(8,128)(2,1)}) %all-gather.8.cloned.1.call-update) | async-done | bytes 1572880 | tf_op jit(solution)/shard_map/all_gather | solution.py:11
  776.2 198.4 %while.27 = (s32[]{:T(128)}, f32[64,96,128]{2,0,1:T(8,128)}, f32[64,48,128]{2,0,1:T(8,128)}, s32[]{:T(128)}, s32[576]{0:T(1024)S(1)}, /*index=5*/s32[]{:T(128)},...) while((s32[]{:T(128)}, f32[64,96,128]{2,0,1:T(8,128)}, ...), condition=%wide.region_13.14_spmd.clone, body=%wide.region_10.13_spmd.clone.sunk | while | flops 272632704 | bytes 27274384 | solution.py:41
  782.0 9.0 scatter_fusion.2
  795.5 9.0 scatter_fusion.3
  810.4 9.0 scatter_fusion.2
  823.9 9.0 scatter_fusion.3
  838.7 9.0 scatter_fusion.2
  852.2 9.0 scatter_fusion.3
  867.0 9.0 scatter_fusion.2
  880.5 9.0 scatter_fusion.3
  895.3 9.0 scatter_fusion.2
  908.9 9.0 scatter_fusion.3
  923.6 9.1 scatter_fusion.2
  937.2 9.0 scatter_fusion.3
  952.0 9.0 scatter_fusion.2
  965.5 9.0 scatter_fusion.3
  981.7 80.2 %reduce-scatter.11.cloned.1.call-done = f32[64,768]{1,0:T(8,128)} async-done(((f32[64,6144]{1,0:T(8,128)}), f32[64,768]{1,0:T(8,128)}) %reduce-scatter.11.cloned.1.call-update) | async-done | bytes 196624 | tf_op jit(solution)/shard_map/reduce_scatter | solution.py:45
  1061.9 79.4 %reduce-scatter.9.cloned.1.call-done = f32[64,768]{1,0:T(8,128)} async-done(((f32[64,12288]{1,0:T(8,128)}), f32[64,768]{1,0:T(8,128)}) %reduce-scatter.9.cloned.1.call-update) | async-done | bytes 196624 | tf_op jit(solution)/shard_map/reduce_scatter | solution.py:42
  1143.7 148.1 %all-reduce.3.cloned.1.call-done = (f32[192,192]{1,0:T(8,128)}, f32[192,192]{1,0:T(8,128)}) async-done(((f32[192,192]{1,0:T(8,128)}, f32[192,192]{1,0:T(8,128)}), (f32[192,192]{1,0:T(8,128)}, f32[192,192]{1,0:T(8,128)})) %all-reduce.3.cloned.1.call-update) | async-done | bytes 294928 | tf_op jit(solution)/shard_map/psum | solution.py:84
  (159 shorter events, 147.3 us)
Async XLA Ops:
  7.2 0.9 copy-start
  7.2 85.8 %copy-start.8 = (s32[1,1,576]{2,1,0:T(1,128)S(1)}, s32[1,1,576]{2,1,0:T(1,128)}, u32[]{:S(2)}) copy-start(s32[1,1,576]{2,1,0:T(1,128)} %param.12) | copy-start | bytes 6916
  7.2 85.8 %copy-start.9 = (s32[1,1,576]{2,1,0:T(1,128)S(1)}, s32[1,1,576]{2,1,0:T(1,128)}, u32[]{:S(2)}) copy-start(s32[1,1,576]{2,1,0:T(1,128)} %param.13) | copy-start | bytes 6916
  7.2 105.7 %all-gather.4.cloned.1.call-start = ((), (), s32[]{:S(2)}) async-start(), calls=%async_computation.4 | async-start | bytes 1769472 | tf_op jit(solution)/shard_map/all_gather | solution.py:12
  91.5 71.8 %all-gather.6.cloned.1.call-start = ((), (), s32[]{:S(2)}) async-start(), calls=%async_computation.5 | async-start | bytes 3342336 | tf_op jit(solution)/shard_map/all_gather | solution.py:11
  92.3 484.5 %reduce-scatter.7.cloned.1.call-start = ((), (), s32[]{:S(2)}) async-start(), calls=%async_computation.7 | async-start | bytes 3538944 | tf_op jit(solution)/shard_map/reduce_scatter | solution.py:45
  464.2 198.0 %reduce-scatter.5.cloned.1.call-start = ((), (), s32[]{:S(2)}) async-start(), calls=%async_computation.6 | async-start | bytes 6684672 | tf_op jit(solution)/shard_map/reduce_scatter | solution.py:42
  470.3 299.4 %all-gather.8.cloned.1.call-start = ((), (), s32[]{:S(2)}) async-start(), calls=%async_computation.8 | async-start | bytes 1671168 | tf_op jit(solution)/shard_map/all_gather | solution.py:11
  663.3 109.5 %copy-start.3 = (f32[128,768]{1,0:T(8,128)}, f32[128,768]{1,0:T(8,128)S(1)}, u32[]{:S(2)}) copy-start(f32[128,768]{1,0:T(8,128)S(1)} %add.116) | copy-start | bytes 1179652
  730.3 331.6 %reduce-scatter.11.cloned.1.call-start = ((), (), s32[]{:S(2)}) async-start(), calls=%async_computation.10 | async-start | bytes 1769472 | tf_op jit(solution)/shard_map/reduce_scatter | solution.py:45
  974.6 2.9 copy-start.2
  977.4 163.9 %reduce-scatter.9.cloned.1.call-start = ((), (), s32[]{:S(2)}) async-start(), calls=%async_computation.9 | async-start | bytes 3342336 | tf_op jit(solution)/shard_map/reduce_scatter | solution.py:42
  979.3 0.9 copy-start.5
  979.3 1.0 copy-start.6
  979.3 2.3 copy-start.4
  979.3 312.4 %all-reduce.3.cloned.1.call-start = ((), (), s32[]{:S(2)}) async-start(), calls=%async_computation.11 | async-start | bytes 786432 | tf_op jit(solution)/shard_map/psum | solution.py:84
  980.3 314.7 %copy-start.1 = (f32[64,768]{1,0:T(8,128)S(1)}, f32[64,768]{1,0:T(8,128)}, u32[]{:S(2)}) copy-start(f32[64,768]{1,0:T(8,128)} %param.10) | copy-start | bytes 589828
  1142.3 152.7 %copy-start.7 = (f32[64,768]{1,0:T(8,128)}, f32[64,768]{1,0:T(8,128)S(1)}, u32[]{:S(2)}) copy-start(f32[64,768]{1,0:T(8,128)S(1)} %add.117) | copy-start | bytes 589828
Sparse Core Ops, SparseCore 0:
  91.7 21.1 all-gather.3
  115.6 47.6 all-gather.5
  464.3 112.4 reduce-scatter.6
  580.0 82.0 reduce-scatter.4
  730.4 39.2 all-gather.7
  977.5 84.3 reduce-scatter.10
  1065.2 76.0 reduce-scatter.8
  1146.6 145.1 all-reduce.2
where the time goes:
time: 1310 us; the launch traced here: 1300 us
  waiting for transfers between devices  591 us (45%)
  other arithmetic  309 us (24%)
  blocking collectives  149 us (11%)
  local copies, waits for them, and re-layouts  118 us (9%)
  matrix products  118 us (9%)
  between operations  15 us (1%)
    reduce_scatter x2, waiting for transfers between devices, apply_graph(): lax.psum_scatter(col_totals.reshape(vec_width, -1), 'row', scatter_dimens...  187 us
    reduce_scatter x2, waiting for transfers between devices, apply_graph(): lax.psum_scatter(row_totals.reshape(vec_width, -1), 'col', scatter_dimens...  165 us
    scatter-add x14, other arithmetic, turn(): row_totals.at[:, row_index].add(forward)  158 us
    psum x1, waiting for transfers between devices, per_device(): lax.psum((product(basis, images), product(basis, basis)), ('row', 'col'))  148 us
    scatter-add x14, other arithmetic, turn(): col_totals.at[:, col_index].add(backward)  125 us
    all_gather x2, waiting for transfers between devices, apply_graph(): row_range = lax.all_gather(vectors, 'col', axis=1, tiled=True)  71.4 us
    psum x1, blocking collectives, per_device(): gram_x = lax.psum(product(block_x, block_x), ('row', 'col'))  68.9 us
    psum x1, blocking collectives, per_device(): rayleigh = lax.psum(product(orthonormal, image_x), ('row', 'col'))  65.7 us
  transfers between devices with their start and end apart: 8, of which 8 were waited for; matrix products, arithmetic and copies ran while one was open for 1% of the time, Pallas kernels for 0%

commit v1 on v0

--- a/solution.py
+++ b/solution.py
@@ -81,7 +81,9 @@
     image_r = apply_graph(residual_low, slot_rows, slot_cols, live_count, slot_vals)
     basis = jnp.concatenate([orthonormal, residual, block_p], axis=0)
     images = jnp.concatenate([image_x, image_r, image_p], axis=0)
-    gram_a, gram_b = lax.psum((product(basis, images), product(basis, basis)), ("row", "col"))
+    gram_a, gram_b = lax.psum(
+        lax.psum((product(basis, images), product(basis, basis)), "col"), "row"
+    )
     return (residual, image_r, gram_a, gram_b)
 
 

time: 1310 us -> 1330 us (1.015)
  other arithmetic: 309 us -> 325 us
    and x14, other arithmetic: 1.14 us -> 14.6 us  [turn(): row_inputs = jnp.take(row_blocks, row_index, axis=1)]
    psum x1 -> x2, waiting for transfers between devices: 148 us -> 146 us  [the longest x1 84.4 us: per_device(): lax.psum((product(basis, images), product(basis, basis)), 'col')]
  transfers between devices with their start and end apart: 8 -> 9, of which waited for: 8 -> 9; matrix products, arithmetic and copies ran while one was open for 1% -> 1% of each run, Pallas kernels for 0% -> 0%
where the time goes in v1:
time: 1330 us; the launch traced here: 1320 us
  waiting for transfers between devices  593 us (45%)
  other arithmetic  325 us (24%)
  blocking collectives  149 us (11%)
  matrix products  119 us (9%)
  local copies, waits for them, and re-layouts  118 us (9%)
  between operations  14.7 us (1%)
    reduce_scatter x2, waiting for transfers between devices, apply_graph(): lax.psum_scatter(col_totals.reshape(vec_width, -1), 'row', scatter_dimens...  191 us
    reduce_scatter x2, waiting for transfers between devices, apply_graph(): lax.psum_scatter(row_totals.reshape(vec_width, -1), 'col', scatter_dimens...  165 us
    scatter-add x14, other arithmetic, turn(): row_totals.at[:, row_index].add(forward)  160 us
    scatter-add x14, other arithmetic, turn(): col_totals.at[:, col_index].add(backward)  125 us
    psum x1, waiting for transfers between devices, per_device(): lax.psum((product(basis, images), product(basis, basis)), 'col')  84.4 us
    all_gather x2, waiting for transfers between devices, apply_graph(): row_range = lax.all_gather(vectors, 'col', axis=1, tiled=True)  71.3 us
    psum x1, blocking collectives, per_device(): gram_x = lax.psum(product(block_x, block_x), ('row', 'col'))  68.9 us
    psum x1, blocking collectives, per_device(): rayleigh = lax.psum(product(orthonormal, image_x), ('row', 'col'))  65.7 us
  transfers between devices with their start and end apart: 9, of which 9 were waited for; matrix products, arithmetic and copies ran while one was open for 1% of the time, Pallas kernels for 0%

profile of v1, /device:TPU:1, one launch (start us, length us, event | category | flops | bytes accessed | tf_op | source)
XLA Modules:
  0.0 1320.4 jit_solution(5548266342379263663)
XLA Ops:
  8.4 68.9 %psum.42 = f32[64,64]{0,1:T(8,128)S(1)} all-reduce(f32[64,64]{0,1:T(8,128)S(1)} %convolution_multiply_fusion.3), channel_id=1, replica_groups=mesh['row'=8,'col'=16] {'row','col'}, use_global_device_ids=true, to_apply=%region_0.0 | all-reduce | flops 4096 | bytes 32768 | tf_op jit(solution)/shard_map/psum | solution.py:66
  77.4 5.8 cholesky.16
  84.6 4.9 custom-call.6
  93.6 19.2 %all-gather.4.cloned.1.call-done = bf16[128,6144]{1,0:T(8,128)(2,1)} async-done(((bf16[128,768]{1,0:T(8,128)(2,1)}), bf16[128,6144]{1,0:T(8,128)(2,1)}) %all-gather.4.cloned.1.call-update) | async-done | bytes 1572880 | tf_op jit(solution)/shard_map/all_gather | solution.py:12
  115.8 47.5 %all-gather.6.cloned.1.call-done = bf16[128,12288]{1,0:T(8,128)(2,1)} async-done(((bf16[128,768]{1,0:T(8,128)(2,1)}), bf16[128,12288]{1,0:T(8,128)(2,1)}) %all-gather.6.cloned.1.call-update) | async-done | bytes 3145744 | tf_op jit(solution)/shard_map/all_gather | solution.py:11
  163.3 4.5 copy_bitcast_fusion.3
  171.6 295.8 %while.26 = (s32[]{:T(128)}, f32[128,96,128]{2,0,1:T(8,128)}, f32[128,48,128]{2,0,1:T(8,128)S(1)}, s32[]{:T(128)}, s32[576]{0:T(1024)S(1)}, /*index=5*/s32[]{:T(...) while((s32[]{:T(128)}, f32[128,96,128]{2,0,1:T(8,128)}, ...), condition=%wide.region_6.7_spmd.clone, body=%wide.region_3.6_spmd.clone.sunk | while | flops 543165312 | bytes 50343056 | solution.py:41
  176.6 5.8 fusion.80
  182.4 13.7 %scatter_fusion = f32[128,96,128]{2,0,1:T(8,128)} fusion(f32[128,96,128]{2,0,1:T(8,128)} %get-tuple-element.409, s32[64]{0:T(128)S(1)} %get-tuple-element.376, f32[64,128,128]{2,1,0:T(8,128)} %fusion.80), kind=kCustom, calls=%fused_computation.4.clone.clone.1 | custom fusion | flops 1048576 | bytes 12583168 | tf_op jit(solution)/shard_map/while/body/scatter-add | solution.py:37
  196.1 4.0 gather_fusion.1
  200.1 4.9 fusion.81
  205.0 8.8 scatter_fusion.1
  218.8 5.8 fusion.80
  224.6 13.7 %scatter_fusion = f32[128,96,128]{2,0,1:T(8,128)} fusion(f32[128,96,128]{2,0,1:T(8,128)} %get-tuple-element.409, s32[64]{0:T(128)S(1)} %get-tuple-element.376, f32[64,128,128]{2,1,0:T(8,128)} %fusion.80), kind=kCustom, calls=%fused_computation.4.clone.clone.1 | custom fusion | flops 1048576 | bytes 12583168 | tf_op jit(solution)/shard_map/while/body/scatter-add | solution.py:37
  242.3 4.9 fusion.81
  247.3 8.8 scatter_fusion.1
  261.1 5.8 fusion.80
  266.9 13.7 %scatter_fusion = f32[128,96,128]{2,0,1:T(8,128)} fusion(f32[128,96,128]{2,0,1:T(8,128)} %get-tuple-element.409, s32[64]{0:T(128)S(1)} %get-tuple-element.376, f32[64,128,128]{2,1,0:T(8,128)} %fusion.80), kind=kCustom, calls=%fused_computation.4.clone.clone.1 | custom fusion | flops 1048576 | bytes 12583168 | tf_op jit(solution)/shard_map/while/body/scatter-add | solution.py:37
  280.6 4.0 gather_fusion.1
  284.6 4.9 fusion.81
  289.5 8.8 scatter_fusion.1
  303.3 5.8 fusion.80
  309.1 13.6 %scatter_fusion = f32[128,96,128]{2,0,1:T(8,128)} fusion(f32[128,96,128]{2,0,1:T(8,128)} %get-tuple-element.409, s32[64]{0:T(128)S(1)} %get-tuple-element.376, f32[64,128,128]{2,1,0:T(8,128)} %fusion.80), kind=kCustom, calls=%fused_computation.4.clone.clone.1 | custom fusion | flops 1048576 | bytes 12583168 | tf_op jit(solution)/shard_map/while/body/scatter-add | solution.py:37
  322.8 4.0 gather_fusion.1
  326.8 4.9 fusion.81
  331.7 8.8 scatter_fusion.1
  345.5 5.8 fusion.80
  351.3 13.8 %scatter_fusion = f32[128,96,128]{2,0,1:T(8,128)} fusion(f32[128,96,128]{2,0,1:T(8,128)} %get-tuple-element.409, s32[64]{0:T(128)S(1)} %get-tuple-element.376, f32[64,128,128]{2,1,0:T(8,128)} %fusion.80), kind=kCustom, calls=%fused_computation.4.clone.clone.1 | custom fusion | flops 1048576 | bytes 12583168 | tf_op jit(solution)/shard_map/while/body/scatter-add | solution.py:37
  365.1 4.0 gather_fusion.1
  369.1 4.9 fusion.81
  374.1 8.8 scatter_fusion.1
  387.9 5.8 fusion.80
  393.7 13.7 %scatter_fusion = f32[128,96,128]{2,0,1:T(8,128)} fusion(f32[128,96,128]{2,0,1:T(8,128)} %get-tuple-element.409, s32[64]{0:T(128)S(1)} %get-tuple-element.376, f32[64,128,128]{2,1,0:T(8,128)} %fusion.80), kind=kCustom, calls=%fused_computation.4.clone.clone.1 | custom fusion | flops 1048576 | bytes 12583168 | tf_op jit(solution)/shard_map/while/body/scatter-add | solution.py:37
  411.4 4.9 fusion.81
  416.3 8.8 scatter_fusion.1
  430.1 5.8 fusion.80
  435.9 13.7 %scatter_fusion = f32[128,96,128]{2,0,1:T(8,128)} fusion(f32[128,96,128]{2,0,1:T(8,128)} %get-tuple-element.409, s32[64]{0:T(128)S(1)} %get-tuple-element.376, f32[64,128,128]{2,1,0:T(8,128)} %fusion.80), kind=kCustom, calls=%fused_computation.4.clone.clone.1 | custom fusion | flops 1048576 | bytes 12583168 | tf_op jit(solution)/shard_map/while/body/scatter-add | solution.py:37
  453.6 4.9 fusion.81
  458.5 8.8 scatter_fusion.1
  469.4 6.1 copy_bitcast_fusion
  475.5 107.7 %reduce-scatter.7.cloned.1.call-done = f32[128,768]{1,0:T(8,128)} async-done(((f32[128,6144]{1,0:T(8,128)}), f32[128,768]{1,0:T(8,128)}) %reduce-scatter.7.cloned.1.call-update) | async-done | bytes 393232 | tf_op jit(solution)/shard_map/reduce_scatter | solution.py:45
  583.2 85.6 %reduce-scatter.5.cloned.1.call-done = f32[128,768]{1,0:T(8,128)} async-done(((f32[128,12288]{1,0:T(8,128)}), f32[128,768]{1,0:T(8,128)}) %reduce-scatter.5.cloned.1.call-update) | async-done | bytes 393232 | tf_op jit(solution)/shard_map/reduce_scatter | solution.py:42
  670.3 65.7 %psum.43 = f32[64,64]{0,1:T(8,128)S(1)} all-reduce(f32[64,64]{0,1:T(8,128)S(1)} %convolution_multiply_fusion.2), channel_id=1, replica_groups=mesh['row'=8,'col'=16] {'row','col'}, use_global_device_ids=true, to_apply=%region_9.10 | all-reduce | flops 4096 | bytes 32768 | tf_op jit(solution)/shard_map/psum | solution.py:76
  737.0 14.5 %all_gather.14 = bf16[64,6144]{1,0:T(8,128)(2,1)S(1)} all-gather(bf16[64,768]{1,0:T(8,128)(2,1)} %get-tuple-element.252), channel_id=1, replica_groups=mesh['row'=8,'col'=16] {'row'}, dimensions={1}, use_global_device_ids=true | all-gather | bytes 884736 | tf_op jit(solution)/shard_map/all_gather | solution.py:12
  752.6 23.9 %all-gather.8.cloned.1.call-done = bf16[64,12288]{1,0:T(8,128)(2,1)} async-done(((bf16[64,768]{1,0:T(8,128)(2,1)}), bf16[64,12288]{1,0:T(8,128)(2,1)}) %all-gather.8.cloned.1.call-update) | async-done | bytes 1572880 | tf_op jit(solution)/shard_map/all_gather | solution.py:11
  782.8 208.8 %while.27 = (s32[]{:T(128)}, f32[64,96,128]{2,0,1:T(8,128)}, f32[64,48,128]{2,0,1:T(8,128)}, s32[]{:T(128)}, s32[576]{0:T(1024)S(1)}, /*index=5*/s32[]{:T(128)},...) while((s32[]{:T(128)}, f32[64,96,128]{2,0,1:T(8,128)}, ...), condition=%wide.region_13.14_spmd.clone, body=%wide.region_10.13_spmd.clone.sunk | while | flops 272632704 | bytes 27293320 | solution.py:41
  789.9 9.1 scatter_fusion.2
  803.5 9.1 scatter_fusion.3
  819.7 9.2 scatter_fusion.2
  833.4 9.2 scatter_fusion.3
  849.7 9.1 scatter_fusion.2
  863.4 9.2 scatter_fusion.3
  879.6 9.1 scatter_fusion.2
  893.2 9.1 scatter_fusion.3
  909.4 9.1 scatter_fusion.2
  923.0 9.1 scatter_fusion.3
  939.2 9.1 scatter_fusion.2
  952.9 9.1 scatter_fusion.3
  969.0 9.1 scatter_fusion.2
  982.6 9.1 scatter_fusion.3
  998.7 83.6 %reduce-scatter.11.cloned.1.call-done = f32[64,768]{1,0:T(8,128)} async-done(((f32[64,6144]{1,0:T(8,128)}), f32[64,768]{1,0:T(8,128)}) %reduce-scatter.11.cloned.1.call-update) | async-done | bytes 196624 | tf_op jit(solution)/shard_map/reduce_scatter | solution.py:45
  1082.3 79.0 %reduce-scatter.9.cloned.1.call-done = f32[64,768]{1,0:T(8,128)} async-done(((f32[64,12288]{1,0:T(8,128)}), f32[64,768]{1,0:T(8,128)}) %reduce-scatter.9.cloned.1.call-update) | async-done | bytes 196624 | tf_op jit(solution)/shard_map/reduce_scatter | solution.py:42
  1164.8 84.4 %all-reduce.5.cloned.1.call-done = (f32[192,192]{1,0:T(8,128)}, f32[192,192]{1,0:T(8,128)}) async-done(((f32[192,192]{1,0:T(8,128)}, f32[192,192]{1,0:T(8,128)}), (f32[192,192]{1,0:T(8,128)}, f32[192,192]{1,0:T(8,128)})) %all-reduce.5.cloned.1.call-update) | async-done | bytes 294928 | tf_op jit(solution)/shard_map/psum | solution.py:85
  1249.2 61.4 %all-reduce.7.cloned.1.call-done = (f32[192,192]{1,0:T(8,128)}, f32[192,192]{1,0:T(8,128)}) async-done(((f32[192,192]{1,0:T(8,128)}, f32[192,192]{1,0:T(8,128)}), (f32[192,192]{1,0:T(8,128)}, f32[192,192]{1,0:T(8,128)})) %all-reduce.7.cloned.1.call-update) | async-done | bytes 294928 | tf_op jit(solution)/shard_map/psum | solution.py:84
  (190 shorter events, 166.2 us)
Async XLA Ops:
  7.2 0.9 copy-start
  7.2 85.8 %copy-start.10 = (s32[1,1,576]{2,1,0:T(1,128)S(1)}, s32[1,1,576]{2,1,0:T(1,128)}, u32[]{:S(2)}) copy-start(s32[1,1,576]{2,1,0:T(1,128)} %param.12) | copy-start | bytes 6916
  7.2 85.8 %copy-start.11 = (s32[1,1,576]{2,1,0:T(1,128)S(1)}, s32[1,1,576]{2,1,0:T(1,128)}, u32[]{:S(2)}) copy-start(s32[1,1,576]{2,1,0:T(1,128)} %param.13) | copy-start | bytes 6916
  7.2 105.7 %all-gather.4.cloned.1.call-start = ((), (), s32[]{:S(2)}) async-start(), calls=%async_computation.4 | async-start | bytes 1769472 | tf_op jit(solution)/shard_map/all_gather | solution.py:12
  91.5 71.8 %all-gather.6.cloned.1.call-start = ((), (), s32[]{:S(2)}) async-start(), calls=%async_computation.5 | async-start | bytes 3342336 | tf_op jit(solution)/shard_map/all_gather | solution.py:11
  92.3 490.9 %reduce-scatter.7.cloned.1.call-start = ((), (), s32[]{:S(2)}) async-start(), calls=%async_computation.7 | async-start | bytes 3538944 | tf_op jit(solution)/shard_map/reduce_scatter | solution.py:45
  469.3 199.5 %reduce-scatter.5.cloned.1.call-start = ((), (), s32[]{:S(2)}) async-start(), calls=%async_computation.6 | async-start | bytes 6684672 | tf_op jit(solution)/shard_map/reduce_scatter | solution.py:42
  475.5 301.0 %all-gather.8.cloned.1.call-start = ((), (), s32[]{:S(2)}) async-start(), calls=%async_computation.8 | async-start | bytes 1671168 | tf_op jit(solution)/shard_map/all_gather | solution.py:11
  670.0 109.5 %copy-start.3 = (f32[128,768]{1,0:T(8,128)}, f32[128,768]{1,0:T(8,128)S(1)}, u32[]{:S(2)}) copy-start(f32[128,768]{1,0:T(8,128)S(1)} %add.120) | copy-start | bytes 1179652
  736.9 259.6 %copy-start.6 = (f32[64,768]{1,0:T(8,128)}, f32[64,768]{1,0:T(8,128)S(1)}, u32[]{:S(2)}) copy-start(f32[64,768]{1,0:T(8,128)S(1)} %get-tuple-element.478) | copy-start | bytes 589828
  737.0 345.4 %reduce-scatter.11.cloned.1.call-start = ((), (), s32[]{:S(2)}) async-start(), calls=%async_computation.10 | async-start | bytes 1769472 | tf_op jit(solution)/shard_map/reduce_scatter | solution.py:45
  782.8 3.2 copy-start.8
  803.5 9.2 copy-start.9
  812.7 3.2 copy-start.8
  833.4 9.2 copy-start.9
  842.6 3.2 copy-start.8
  863.4 9.2 copy-start.9
  872.5 3.2 copy-start.8
  893.2 9.1 copy-start.9
  902.4 3.2 copy-start.8
  923.0 9.1 copy-start.9
  932.2 3.2 copy-start.8
  952.8 9.1 copy-start.9
  961.9 3.2 copy-start.8
  982.6 9.1 copy-start.9
  991.7 2.9 copy-start.2
  994.5 166.8 %reduce-scatter.9.cloned.1.call-start = ((), (), s32[]{:S(2)}) async-start(), calls=%async_computation.9 | async-start | bytes 3342336 | tf_op jit(solution)/shard_map/reduce_scatter | solution.py:42
  996.4 0.9 copy-start.5
  996.4 2.3 copy-start.4
  996.5 252.7 %all-reduce.5.cloned.1.call-start = ((), (), s32[]{:S(2)}) async-start(), calls=%async_computation.11 | async-start | bytes 786432 | tf_op jit(solution)/shard_map/psum | solution.py:85
  998.7 315.2 %copy-start.1 = (f32[64,768]{1,0:T(8,128)S(1)}, f32[64,768]{1,0:T(8,128)}, u32[]{:S(2)}) copy-start(f32[64,768]{1,0:T(8,128)} %param.10) | copy-start | bytes 589828
  1162.4 151.5 %copy-start.7 = (f32[64,768]{1,0:T(8,128)}, f32[64,768]{1,0:T(8,128)S(1)}, u32[]{:S(2)}) copy-start(f32[64,768]{1,0:T(8,128)S(1)} %add.121) | copy-start | bytes 589828
  1164.8 145.9 %all-reduce.7.cloned.1.call-start = ((), (), s32[]{:S(2)}) async-start(), calls=%async_computation.12 | async-start | bytes 786432 | tf_op jit(solution)/shard_map/psum | solution.py:84
Sparse Core Ops, SparseCore 0:
  91.7 21.1 all-gather.3
  115.6 47.6 all-gather.5
  469.5 113.6 reduce-scatter.6
  586.5 82.2 reduce-scatter.4
  737.1 39.3 all-gather.7
  994.6 87.6 reduce-scatter.10
  1085.6 75.6 reduce-scatter.8
  1165.2 83.9 all-reduce.4
  1251.6 58.9 all-reduce.6
